TPU v7x, 32 devices: a whole 2x2x4 slice. The times are simulated.
32 devices in a mesh: row: 4 (over y, core), col: 8 (over z, x).
Axes of the slice: x: 2, y: 2, z: 4, core: 2. Of those that a mesh axis runs over, the one named last changes fastest.
Arguments:
- solution: float32 [4, 8, 16, 128, 128], P('row', 'col'), may hold values from -6 to 6
- residual: float32 [4, 8, 16, 128, 128], P('row', 'col'), may hold values from -6 to 6, as said below
- prev_direction: float32 [4, 8, 16, 128, 128], P('row', 'col'), may hold values from -6 to 6, as said below
- prev_dot: float32 [128], replicated, may hold values from 32768 to 131072
- face_lists: int32 [4, 8, 4, 4], P('row', 'col'), may hold values from 0 to 16, as said below
- multiplicity: int32 [4, 8, 16], P('row', 'col'), may hold values from 1 to 2, as said below
- block_pattern: int32 [4, 8, 16, 3], P('row', 'col'), may hold values from 0 to 15, as said below
- schur: float32 [4, 8, 16, 3, 128, 128], P('row', 'col'), may hold values from -1 to 4, as said below
- neumann_inverse: float32 [4, 8, 16, 3, 128, 128], P('row', 'col'), may hold values from 0 to 2, as said below
- coarse_basis: float32 [4, 8, 8, 2048], P('row', 'col'), may hold values from -0.25 to 0.25
- primal_map: int32 [4, 8, 8], P('row', 'col'), may hold values from 0 to 255, all different within a row
- coarse_inverse: float32 [256, 256], P('col'), may hold values from -1 to 1, as said below
Outputs:
- new_solution: float32 [4, 8, 16, 128, 128], P('row', 'col')
- new_residual: float32 [4, 8, 16, 128, 128], P('row', 'col')
- direction: float32 [4, 8, 16, 128, 128], P('row', 'col')
Inputs may be any that keep to these rules, and one draw needn't show every extreme that they name: face_lists[i, j, f, k] names the interface blocks that subdomain (i, j) shares with its neighbour across face f (0 toward row i-1, 1 toward row i+1, 2 toward column j-1, 3 toward column j+1); slot k of a face names the same unknowns as slot k of the neighbour's list for the facing face, and both lists have the same length, 1 to 4 blocks, none on faces at the grid's edge; unused slots hold 16; no block lies on two faces; some face holds 4 blocks. multiplicity is 2 for blocks named in face_lists and 1 for the others. block_pattern[i, j, b, 0] = b; the two other entries of block row b are two other blocks, each of which lists b in turn. `schur`: each subdomain's Schur complement is symmetric positive definite, with positive diagonal and no positive entry off it. `neumann_inverse`: each subdomain's local solve matrix is symmetric positive definite. `coarse_inverse`: symmetric positive definite. `residual`: copies of an unknown held by two subdomains (slot k of facing lists) are equal. `prev_direction`: copies of an unknown held by two subdomains (slot k of facing lists) are equal.
All inputs are finite; a program needn't handle non-finite values.
Results may differ from a plain program's by a relative error of at most 0.0003.
Values sent between devices are 32-bit elements; how exact they have to be, the bound alone decides.
No kernel may reach another device: no remote copies, remote signals or barrier semaphores. Data moves between devices by JAX's collectives and lax.ppermute only.
A program may use at most 128 MiB of HBM per device.

v0:
```python
import jax
import jax.numpy as jnp
from jax import lax
from jax.experimental import pallas as pl
from jax.experimental.pallas import tpu as pltpu
from jax.sharding import PartitionSpec as P

F32 = jnp.float32
BF16 = jnp.bfloat16
SLOTS = 4
HEAD = 10
SMEM = pl.BlockSpec(memory_space=pltpu.SMEM)
VMEM = pl.BlockSpec(memory_space=pltpu.VMEM)
HBM = pl.BlockSpec(memory_space=pltpu.HBM)
ANY = pl.BlockSpec(memory_space=pl.ANY)


def halves(x):
    high = x.astype(BF16)
    return high, (x - high.astype(F32)).astype(BF16)


def dot(a, b):
    return jnp.dot(a, b, preferred_element_type=F32)


def dot_first(a, b):
    return lax.dot_general(a, b, (((0,), (0,)), ((), ())), preferred_element_type=F32)


def fold(x):
    width = x.shape[1] // 2
    return x[:, :width] + x[:, width:]


def product(matrix, pair):
    high, low = halves(matrix)
    return fold(dot(high, pair)) + dot(low, pair[:, : pair.shape[1] // 2])


def exact_pair(x):
    return jnp.concatenate(halves(x), axis=1)


def halved_rows(row_blocks):
    matrix = jnp.concatenate([row_blocks[k] for k in range(3)], axis=1)
    return jnp.concatenate(halves(matrix), axis=0)


def row_product(stacked, pattern, b, pairs):
    field = jnp.concatenate([pairs[pattern[k, 0, b]] for k in range(3)], axis=0)
    both = fold(dot(stacked, field))
    return both[:128] + both[128:]


def partial_rows(x):
    rows, cols = x.shape
    return jnp.sum(x.reshape(rows // 8, 8, cols), axis=0)


def weight_of(multiplicity, b):
    return 1.0 / jnp.full((1, 128), multiplicity[b].astype(F32))


def mapped(primal_map, shape, dim):
    place = lax.broadcasted_iota(jnp.int32, shape, dim)
    found = jnp.zeros(shape, jnp.int32)
    for p in range(8):
        found = jnp.where(place == p, primal_map[p], found)
    return found


def row_index():
    return 2 * lax.axis_index("y") + lax.axis_index("core")


def partner_faces():
    row, col = lax.axis_index("core"), lax.axis_index("col") % 2
    return 1 - row, row, 3 - col, 2 + col


def slots_by_block(faces, slot):
    for b in range(17):
        slot[b] = 16
    for s, f in enumerate(partner_faces()):
        for k in range(SLOTS):
            slot[faces[f, k]] = s * SLOTS + k


def local_kernel(
    faces_hbm, multiplicity_hbm, pattern_hbm, primal_map_hbm, residual_hbm, neumann_hbm, basis_hbm, inverse_hbm,
    local, send_2, told_hbm, send_1, send_0, send_3,
    faces, multiplicity, pattern, primal_map, residual, neumann, basis, inverse, pairs, told,
    index_sems, residual_sem, neumann_sems, basis_sems, told_sem,
):
    count = residual.shape[0]
    index_copies = [
        pltpu.make_async_copy(source, target, index_sems.at[i])
        for i, (source, target) in enumerate(
            ((multiplicity_hbm, multiplicity), (pattern_hbm, pattern), (primal_map_hbm, primal_map), (faces_hbm, faces))
        )
    ]
    basis_copy = pltpu.make_async_copy(basis_hbm, basis, basis_sems.at[0])
    inverse_copy = pltpu.make_async_copy(inverse_hbm, inverse, basis_sems.at[1])
    residual_copy = pltpu.make_async_copy(residual_hbm, residual, residual_sem)
    neumann_copies = {}
    for c, (start, stop) in enumerate(((0, count // 4), (count // 4, count))):
        part = pl.ds(start, stop - start)
        neumann_copies[start] = pltpu.make_async_copy(neumann_hbm.at[part], neumann.at[part], neumann_sems.at[c])
    for copy in (*index_copies, residual_copy, basis_copy, *neumann_copies.values(), inverse_copy):
        copy.start()
    for copy in index_copies:
        copy.wait()
    residual_copy.wait()
    basis_copy.wait()
    for b in range(count):
        pairs[b] = exact_pair(residual[b] * weight_of(multiplicity, b))
    total = jnp.zeros((8, 128), F32)
    for b in range(count):
        if b in neumann_copies:
            neumann_copies[b].wait()
        if b == count // 4:
            coarse_local = product(basis[...], pairs[...].reshape(count * 128, 256))
        weight = weight_of(multiplicity, b)
        out = row_product(halved_rows(neumann.at[b]), pattern, b, pairs) * weight
        local[b] = out
        total += partial_rows(residual[b] * out)
    row = lax.broadcasted_iota(jnp.int32, (8, 128), 0)
    total = jnp.sum(total, axis=0, keepdims=True)
    map_row = mapped(primal_map, (8, 128), 1).astype(F32)
    inverse_copy.wait()
    sharers = inverse.shape[0] // 8
    mine = row_index() % sharers
    share = inverse[pl.ds(pl.multiple_of(mine * 8, 8), 8), :]
    rows = [coarse_local, jnp.where(row == 0, total, map_row)[:2]]
    rows = jnp.concatenate(rows + [share[:, i : i + 128] for i in range(0, inverse.shape[1], 128)], axis=0)
    each = rows.shape[0]
    for i in range(told.shape[0] // each):
        told[each * i : each * i + each, :] = rows
    told_copy = pltpu.make_async_copy(told, told_hbm, told_sem)
    told_copy.start()
    for f, sent in zip(partner_faces(), (send_0, send_1, send_2, send_3)):
        for k in range(SLOTS):
            b = jnp.minimum(faces[f, k], count - 1)
            sent[k * 128 : (k + 1) * 128, :] = local[b]
            lanes = pl.ds(pl.multiple_of(b * 128, 128), 128)
            sent[512 + 8 * k : 520 + 8 * k, :] = basis[:, lanes] * weight_of(multiplicity, b)
    told_copy.wait()


def back(basis, own):
    bh, bl = (h.astype(F32) for h in halves(basis))
    oh, ol = (h.astype(F32) for h in halves(own))
    left = jnp.concatenate([bh, bl, bh, bl], axis=0).astype(BF16)
    right = jnp.concatenate([oh, oh, ol, ol], axis=0).astype(BF16)
    return dot_first(left, right)


def halving_kernel(schur_hbm, stacked, schur, sems):
    count = schur.shape[0]
    copies = []
    for c in range(4):
        part = pl.ds(c * count // 4, count // 4)
        copies.append(pltpu.make_async_copy(schur_hbm.at[part], schur.at[part], sems.at[c]))
        copies[c].start()
    for b in range(count):
        if b % (count // 4) == 0:
            copies[b // (count // 4)].wait()
        stacked[b] = halved_rows(schur.at[b])


def coarse_kernel(
    multiplicity, primal_map, local, same_core, other_core, basis, prev_dot, previous_hbm,
    started, wanted, precond_dot, inverse, previous, previous_sem,
):
    count = local.shape[0]
    previous_copy = pltpu.make_async_copy(previous_hbm, previous, previous_sem)
    previous_copy.start()

    order = inverse.shape[1]
    each = HEAD + 8 * (order // 128)
    half = same_core.shape[0] // each
    cols = lax.axis_size("col")
    sharers = order // cols // 8
    for told, core in ((same_core, lax.axis_index("core")), (other_core, 1 - lax.axis_index("core"))):
        for i in range(half):
            target = pl.multiple_of((i % cols * sharers + (2 * (i // cols) + core) % sharers) * 8, 8)
            for j in range(order // 128):
                source = i * each + HEAD + 8 * j
                inverse[pl.ds(target, 8), 128 * j : 128 * j + 128] = told[source : source + 8, :]

    def row_of_all(p):
        return jnp.concatenate([x[pl.ds(p, half, stride=each), :] for x in (same_core, other_core)], axis=0)

    maps = row_of_all(9).astype(jnp.int32)
    lane = lax.broadcasted_iota(jnp.int32, (2 * half, order), 1)
    chosen = [(maps[:, p : p + 1] == lane).astype(F32) for p in range(8)]
    chosen = jnp.concatenate(chosen, axis=0).astype(BF16)
    rows = jnp.concatenate([row_of_all(p) for p in range(8)], axis=0)
    rhs = fold(dot_first(chosen, exact_pair(rows)))
    coarse = product(inverse[...], exact_pair(rhs))
    dots = jnp.sum(row_of_all(8), axis=0, keepdims=True)
    dots = dots + jnp.sum(rhs * coarse, axis=0, keepdims=True)
    precond_dot[...] = dots
    beta = dots / prev_dot[...]
    y, core, col = (lax.axis_index(name) for name in ("y", "core", "col"))
    odd = col % 2
    partners = (
        (other_core, y * cols + col),
        (other_core, jnp.clip(y + 2 * core - 1, 0, lax.axis_size("y") - 1) * cols + col),
        (same_core, y * cols + (col + 1 - 2 * odd)),
        (same_core, y * cols + jnp.clip(col + 2 * odd - 1, 0, cols - 1)),
    )
    map_rows = [x[pl.ds(i * each + 9, 1), :] for x, i in partners]
    map_rows = jnp.concatenate([jnp.broadcast_to(row, (8, 128)) for row in map_rows], axis=0)
    on_diagonal = lax.broadcasted_iota(jnp.int32, (32, 128), 0) % 8 == lax.broadcasted_iota(jnp.int32, (32, 128), 1)
    maps = jnp.sum(jnp.where(on_diagonal, map_rows, 0.0), axis=1, keepdims=True).astype(jnp.int32)
    maps = jnp.concatenate([mapped(primal_map, (8, 128), 0)[:, 0:1], maps], axis=0)
    lane = lax.broadcasted_iota(jnp.int32, (40, order), 1)
    picked = fold(dot((maps == lane).astype(F32).astype(BF16), exact_pair(coarse)))
    wanted[...] = picked[8:40]
    own_back = back(basis[...], picked[0:8])
    previous_copy.wait()
    for b in range(count):
        mine = local[b] + own_back[b * 128 : (b + 1) * 128] * weight_of(multiplicity, b)
        started[b] = mine + beta * previous[b]
def direction_kernel(
    faces, pattern, started, wanted, got_2, got_1, got_0, got_3, stacked,
    direction_hbm, direction, image, send_2, send_1, send_0, send_3, curvature,
    added, pairs, slot, direction_sem,
):
    count = started.shape[0]
    slots_by_block(faces, slot)
    for s, r in enumerate((got_0, got_1, got_2, got_3)):
        face_basis = jnp.concatenate([r[512 + 8 * k : 520 + 8 * k, :] for k in range(SLOTS)], axis=1)
        face_back = back(face_basis, wanted[8 * s : 8 * s + 8, :])
        for k in range(SLOTS):
            part = slice(k * 128, (k + 1) * 128)
            added[s * SLOTS + k] = r[part, :] + face_back[part]
    added[16] = jnp.zeros((128, 128), F32)
    for b in range(count):
        value = started[b] + added[slot[b]]
        direction[b] = value
        pairs[b] = exact_pair(value)
    direction_copy = pltpu.make_async_copy(direction, direction_hbm, direction_sem)
    direction_copy.start()
    total = jnp.zeros((8, 128), F32)
    for b in range(count):
        out = row_product(stacked[b], pattern, b, pairs)
        image[b] = out
        total += partial_rows(direction[b] * out)
    for f, sent in zip(partner_faces(), (send_0, send_1, send_2, send_3)):
        for k in range(SLOTS):
            sent[k * 128 : (k + 1) * 128, :] = image[jnp.minimum(faces[f, k], count - 1)]
    curvature[...] = jnp.broadcast_to(jnp.sum(total, axis=0, keepdims=True), curvature.shape)
    direction_copy.wait()


def update_kernel(
    faces_any, current, residual, direction, image, got_2, got_1, got_0, got_3, curvature, precond_dot,
    new_solution_hbm, new_residual_hbm,
    faces, new_solution, new_residual, added, slot, faces_sem, solution_sems, residual_sems,
):
    count = current.shape[0]
    faces_copy = pltpu.make_async_copy(faces_any, faces, faces_sem)
    faces_copy.start()
    step = precond_dot[...] / jnp.sum(curvature[...], axis=0, keepdims=True)
    copies = []

    def leave(c, value, value_hbm, sems):
        part = pl.ds(c * count // 4, count // 4)
        copies.append(pltpu.make_async_copy(value.at[part], value_hbm.at[part], sems.at[c]))
        copies[-1].start()

    for b in range(count):
        new_solution[b] = current[b] + step * direction[b]
        if (b + 1) % (count // 4) == 0:
            leave(b // (count // 4), new_solution, new_solution_hbm, solution_sems)
    for s, r in enumerate((got_0, got_1, got_2, got_3)):
        for k in range(SLOTS):
            added[s * SLOTS + k] = r[k * 128 : (k + 1) * 128, :]
    added[16] = jnp.zeros((128, 128), F32)
    faces_copy.wait()
    slots_by_block(faces, slot)
    for b in range(count):
        new_residual[b] = residual[b] - step * (image[b] + added[slot[b]])
        if (b + 1) % (count // 4) == 0:
            leave(b // (count // 4), new_residual, new_residual_hbm, residual_sems)
    for copy in copies:
        copy.wait()


def swap_pairs(x, axis, first):
    pairs = [(i, i + 1) for i in range(first, lax.axis_size(axis) - 1, 2)]
    return lax.ppermute(x, axis, pairs + [(j, i) for i, j in pairs])


def from_all(x, axes):
    sent = x.reshape(lax.axis_size(axes), 1, -1)
    return lax.all_to_all(sent, axes, split_axis=0, concat_axis=0, tiled=True).reshape(x.shape)


def shape(*dims):
    return jax.ShapeDtypeStruct(dims, F32)


def held(*dims):
    return pltpu.VMEM(dims, F32)


def in_hbm(x):
    return pltpu.with_memory_space_constraint(x, pltpu.HBM)


def kernel_params(mib):
    return pltpu.CompilerParams(vmem_limit_bytes=mib << 20)


def per_device(
    solution,
    residual,
    prev_direction,
    prev_dot,
    face_lists,
    multiplicity,
    block_pattern,
    schur,
    neumann_inverse,
    coarse_basis,
    primal_map,
    coarse_inverse,
):
    current, residual, previous = solution[0, 0], residual[0, 0], prev_direction[0, 0]
    faces, multiplicity = face_lists[0, 0], multiplicity[0, 0]
    pattern = jnp.transpose(block_pattern, (0, 3, 1, 2))[0]
    schur, neumann = schur[0, 0], neumann_inverse[0, 0]
    basis, primal_map = coarse_basis[0, 0], primal_map[0, 0]
    count, dofs, cases = residual.shape

    everywhere = lax.axis_size(("y", "core", "col"))
    order = coarse_inverse.shape[1]
    told_rows = (HEAD + 8 * (order // cases)) * (everywhere // 2)

    face = held(SLOTS * dofs + 32, cases)
    indices = (faces, multiplicity, pattern, primal_map)
    local, send_2, told, send_1, send_0, send_3 = pl.pallas_call(
        local_kernel,
        out_shape=(held(count, dofs, cases), face, shape(told_rows, cases), face, face, face),
        in_specs=[HBM] * 8,
        out_specs=(VMEM, VMEM, HBM, VMEM, VMEM, VMEM),
        scratch_shapes=[pltpu.SMEM(x.shape, jnp.int32) for x in indices]
        + [
            pltpu.VMEM(residual.shape, F32),
            pltpu.VMEM(neumann.shape, F32),
            pltpu.VMEM(basis.shape, F32),
            pltpu.VMEM(coarse_inverse.shape, F32),
            pltpu.VMEM((count, dofs, 2 * cases), BF16),
            pltpu.VMEM((told_rows, cases), F32),
            pltpu.SemaphoreType.DMA((4,)),
            pltpu.SemaphoreType.DMA,
            pltpu.SemaphoreType.DMA((2,)),
            pltpu.SemaphoreType.DMA((2,)),
            pltpu.SemaphoreType.DMA,
        ],
        compiler_params=kernel_params(16),
        name="local_solve",
    )(*(in_hbm(x) for x in (*indices, residual, neumann, basis, coarse_inverse)))

    same_core = from_all(told, ("y", "col"))
    other_core = lax.ppermute(same_core, "core", [(0, 1), (1, 0)])
    got_2 = swap_pairs(send_2, "col", 0)
    got_1 = swap_pairs(send_1, ("y", "core"), 1)
    got_0 = swap_pairs(send_0, ("y", "core"), 0)
    got_3 = swap_pairs(send_3, "col", 1)

    stacked = pl.pallas_call(
        halving_kernel,
        out_shape=pltpu.VMEM((count, 2 * dofs, 3 * dofs), BF16),
        in_specs=[HBM],
        out_specs=VMEM,
        scratch_shapes=[pltpu.VMEM(schur.shape, F32), pltpu.SemaphoreType.DMA((4,))],
        compiler_params=kernel_params(12),
        name="halving",
    )(in_hbm(schur))

    started, wanted, precond_dot = pl.pallas_call(
        coarse_kernel,
        out_shape=(held(count, dofs, cases), held(32, cases), held(1, cases)),
        in_specs=[SMEM] * 2 + [VMEM] * 5 + [HBM],
        out_specs=(VMEM,) * 3,
        scratch_shapes=[
            pltpu.VMEM((order, order), F32),
            pltpu.VMEM(previous.shape, F32),
            pltpu.SemaphoreType.DMA,
        ],
        compiler_params=kernel_params(24),
        name="coarse_solve",
    )(
        multiplicity, primal_map, local, same_core, other_core, basis, prev_dot.reshape(1, cases),
        in_hbm(previous),
    )

    direction, direction_held, image, send_2, send_1, send_0, send_3, curvature = pl.pallas_call(
        direction_kernel,
        out_shape=(shape(count, dofs, cases), held(count, dofs, cases), held(count, dofs, cases))
        + (held(SLOTS * dofs, cases),) * 4
        + (held(everywhere, cases),),
        in_specs=[SMEM] * 2 + [VMEM] * 7,
        out_specs=(HBM,) + (VMEM,) * 7,
        scratch_shapes=[
            pltpu.VMEM((17, dofs, cases), F32),
            pltpu.VMEM((count, dofs, 2 * cases), BF16),
            pltpu.SMEM((17,), jnp.int32),
            pltpu.SemaphoreType.DMA,
        ],
        compiler_params=kernel_params(16),
        name="direction_image",
    )(faces, pattern, started, wanted, got_2, got_1, got_0, got_3, stacked)

    got_2 = swap_pairs(send_2, "col", 0)
    got_1 = swap_pairs(send_1, ("y", "core"), 1)
    got_0 = swap_pairs(send_0, ("y", "core"), 0)
    got_3 = swap_pairs(send_3, "col", 1)
    curvature = from_all(curvature, ("y", "core", "col"))

    new_solution, new_residual = pl.pallas_call(
        update_kernel,
        out_shape=(shape(count, dofs, cases),) * 2,
        in_specs=[ANY] + [VMEM] * 10,
        out_specs=(HBM,) * 2,
        scratch_shapes=[
            pltpu.SMEM(faces.shape, jnp.int32),
            pltpu.VMEM(residual.shape, F32),
            pltpu.VMEM(residual.shape, F32),
            pltpu.VMEM((17, dofs, cases), F32),
            pltpu.SMEM((17,), jnp.int32),
            pltpu.SemaphoreType.DMA,
            pltpu.SemaphoreType.DMA((4,)),
            pltpu.SemaphoreType.DMA((4,)),
        ],
        compiler_params=kernel_params(16),
        name="update",
    )(
        faces, current, residual, direction_held, image, got_2, got_1, got_0, got_3, curvature, precond_dot
    )
    return (new_solution[None, None], new_residual[None, None], direction[None, None])


def solution(mesh):
    rows, cols = mesh.devices.shape
    mesh = jax.sharding.Mesh(mesh.devices.reshape(rows // 2, 2, cols), ("y", "core", "col"))
    split = lambda dims: P(("y", "core"), "col", *(None,) * dims)
    placed = (
        split(3), split(3), split(3), P(), split(2), split(1), split(2), split(4), split(4), split(2), split(1),
        P("col", None),
    )
    return jax.shard_map(
        per_device,
        mesh=mesh,
        in_specs=placed,
        out_specs=(split(3), split(3), split(3)),
        check_vma=False,
    )
```

profile of v0, /device:TPU:0, one launch (start us, length us, event | category | flops | bytes accessed | tf_op | source)
XLA Modules:
  0.0 52.2 jit_solution(11809968940817022113)
XLA Ops:
  0.6 4.3 %local_solve.1 = (f32[16,128,128]{2,1,0:T(8,128)S(1)}, f32[544,128]{1,0:T(8,128)S(1)}, f32[416,128]{1,0:T(8,128)}, f32[544,128]{1,0:T(8,128)S(1)}, f32[544,128]{1,0:T(8,128)S(1)}, /*index=5*/f32[544,128]{1,0:T(8,128)S(1)}) custom-call(s32[4,4]{1,0:T(4,128)} %bitcast.30, s32[16]{0:T(128)} %bitcast.36, s32[3,1,16]{2,1,0:T(1,128)} %bitcast.34, s32[8]{0:T(128)} %bitcast.38, ...), custom_call_target="tpu_custom_call" | custom-call | tf_op jit(solution)/shard_map/local_solve/pallas_call | solution.py:346
  5.0 8.3 %all-to-all-start = ((f32[16,1,3328]{2,1,0:T(1,128)}), f32[16,1,3328]{2,1,0:T(1,128)S(1)}, u32[]{:S(2)}, u32[]{:S(2)}) async-start(f32[16,1,3328]{2,1,0:T(1,128)} %bitcast.10), calls=%async_computation | async-start | bytes 425984 | tf_op jit(solution)/shard_map/all_to_all | solution.py:300
  13.3 1.9 %collective-permute-start.1 = (f32[544,128]{1,0:T(8,128)S(1)}, f32[544,128]{1,0:T(8,128)S(1)}, u32[]{:S(2)}, u32[]{:S(2)}) collective-permute-start(f32[544,128]{1,0:T(8,128)S(1)} %get-tuple-element.26), channel_id=1, source_target_pairs={{0,1},{2,3},{4,5},{6,7},{1,0},{3,2},{5,4},{7,6},{8,9},{10,11},{12,... | collective-permute-start | bytes 835592 | tf_op jit(solution)/shard_map/ppermute | solution.py:295
  15.2 0.7 %collective-permute-start.2 = (f32[544,128]{1,0:T(8,128)S(1)}, f32[544,128]{1,0:T(8,128)S(1)}, u32[]{:S(2)}, u32[]{:S(2)}) collective-permute-start(f32[544,128]{1,0:T(8,128)S(1)} %get-tuple-element.27), channel_id=1, source_target_pairs={{8,16},{16,8},{9,17},{17,9},{10,18},{18,10},{11,19},{19,11},{12,20... | collective-permute-start | bytes 835592 | tf_op jit(solution)/shard_map/ppermute | solution.py:295
  15.9 2.9 %collective-permute-start.3 = (f32[544,128]{1,0:T(8,128)S(1)}, f32[544,128]{1,0:T(8,128)S(1)}, u32[]{:S(2)}, u32[]{:S(2)}) collective-permute-start(f32[544,128]{1,0:T(8,128)S(1)} %get-tuple-element.28), channel_id=1, source_target_pairs={{0,8},{16,24},{8,0},{24,16},{1,9},{17,25},{9,1},{25,17},{2,10},{18... | collective-permute-start | bytes 835592 | tf_op jit(solution)/shard_map/ppermute | solution.py:295
  18.8 0.7 %collective-permute-start.4 = (f32[544,128]{1,0:T(8,128)S(1)}, f32[544,128]{1,0:T(8,128)S(1)}, u32[]{:S(2)}, u32[]{:S(2)}) collective-permute-start(f32[544,128]{1,0:T(8,128)S(1)} %get-tuple-element.29), channel_id=1, source_target_pairs={{1,2},{3,4},{5,6},{2,1},{4,3},{6,5},{9,10},{11,12},{13,14},{10,9},... | collective-permute-start | bytes 835592 | tf_op jit(solution)/shard_map/ppermute | solution.py:295
  19.4 2.6 %all-to-all-done = f32[16,1,3328]{2,1,0:T(1,128)S(1)} async-done(((f32[16,1,3328]{2,1,0:T(1,128)}), f32[16,1,3328]{2,1,0:T(1,128)S(1)}, u32[]{:S(2)}, u32[]{:S(2)}) %all-to-all-start) | async-done | bytes 213024 | tf_op jit(solution)/shard_map/all_to_all | solution.py:300
  22.1 0.0 collective-permute-start
  22.1 0.0 copy-start.2
  22.1 0.0 copy-start.5
  22.1 0.0 copy-start.6
  22.1 0.0 copy-start.7
  22.1 0.0 copy-start.3
  22.1 0.0 copy-start.4
  22.1 2.1 %halving.1.stacked = bf16[16,256,384]{2,1,0:T(8,128)(2,1)S(1)} custom-call(f32[16,3,128,128]{3,2,1,0:T(8,128)} %bitcast.41), custom_call_target="tpu_custom_call" | custom-call | tf_op jit(solution)/shard_map/halving/pallas_call | solution.py:376
  24.2 0.0 collective-permute-done.other_core
  24.2 0.0 copy-done.2
  24.2 0.0 copy-done.5
  24.2 0.0 copy-done.6
  24.2 0.0 copy-done.7
  24.2 2.6 %coarse_solve.1 = (f32[16,128,128]{2,1,0:T(8,128)S(1)}, f32[32,128]{1,0:T(8,128)S(1)}, f32[1,128]{1,0:T(1,128)S(1)}) custom-call(s32[16]{0:T(128)S(1)} %bitcast.37, s32[8]{0:T(128)S(1)} %bitcast.39, f32[16,128,128]{2,1,0:T(8,128)S(1)} %get-tuple-element.22.local, f32[416,128]{1,0:T(8,128)S(1)} %bitcast.26, f32[416,128]{1,0:T(8,128)S(1)} %collective-permute-done.other_core, ...), custom_call_target="tpu_custom_call" | custom-call | tf_op jit(solution)/shard_map/coarse_solve/pallas_call | solution.py:386
  26.9 0.0 copy-start
  26.9 0.0 copy-start.1
  26.9 0.0 collective-permute-done.1.got_2
  26.9 0.0 collective-permute-done.2.got_1
  26.9 0.0 collective-permute-done.3.got_0
  26.9 0.0 collective-permute-done.4.got_3
  27.0 0.0 copy-done.3
  27.0 0.0 copy-done.4
  27.0 2.6 %direction_image.1 = (f32[16,128,128]{2,1,0:T(8,128)}, f32[16,128,128]{2,1,0:T(8,128)S(1)}, f32[16,128,128]{2,1,0:T(8,128)S(1)}, f32[512,128]{1,0:T(8,128)S(1)},...) custom-call(s32[4,4]{1,0:T(4,128)S(1)} %bitcast.31, ...), custom_call_target="tpu_custom_call" | custom-call | tf_op jit(solution)/shard_map/direction_image/pallas_call | solution.py:403
  29.5 4.1 %collective-permute-start.5 = (f32[512,128]{1,0:T(8,128)S(1)}, f32[512,128]{1,0:T(8,128)S(1)}, u32[]{:S(2)}, u32[]{:S(2)}) collective-permute-start(f32[512,128]{1,0:T(8,128)S(1)} %get-tuple-element.32), channel_id=1, source_target_pairs={{0,1},{2,3},{4,5},{6,7},{1,0},{3,2},{5,4},{7,6},{8,9},{10,11},{12,... | collective-permute-start | bytes 786440 | tf_op jit(solution)/shard_map/ppermute | solution.py:295
  33.6 0.7 %collective-permute-start.6 = (f32[512,128]{1,0:T(8,128)S(1)}, f32[512,128]{1,0:T(8,128)S(1)}, u32[]{:S(2)}, u32[]{:S(2)}) collective-permute-start(f32[512,128]{1,0:T(8,128)S(1)} %get-tuple-element.33), channel_id=1, source_target_pairs={{8,16},{16,8},{9,17},{17,9},{10,18},{18,10},{11,19},{19,11},{12,20... | collective-permute-start | bytes 786440 | tf_op jit(solution)/shard_map/ppermute | solution.py:295
  34.3 3.0 %collective-permute-start.7 = (f32[512,128]{1,0:T(8,128)S(1)}, f32[512,128]{1,0:T(8,128)S(1)}, u32[]{:S(2)}, u32[]{:S(2)}) collective-permute-start(f32[512,128]{1,0:T(8,128)S(1)} %get-tuple-element.34), channel_id=1, source_target_pairs={{0,8},{16,24},{8,0},{24,16},{1,9},{17,25},{9,1},{25,17},{2,10},{18... | collective-permute-start | bytes 786440 | tf_op jit(solution)/shard_map/ppermute | solution.py:295
  37.2 0.7 %collective-permute-start.8 = (f32[512,128]{1,0:T(8,128)S(1)}, f32[512,128]{1,0:T(8,128)S(1)}, u32[]{:S(2)}, u32[]{:S(2)}) collective-permute-start(f32[512,128]{1,0:T(8,128)S(1)} %get-tuple-element.35), channel_id=1, source_target_pairs={{1,2},{3,4},{5,6},{2,1},{4,3},{6,5},{9,10},{11,12},{13,14},{10,9},... | collective-permute-start | bytes 786440 | tf_op jit(solution)/shard_map/ppermute | solution.py:295
  37.9 12.6 %all_to_all.10 = f32[32,1,128]{2,1,0:T(1,128)S(1)} all-to-all(f32[32,1,128]{2,1,0:T(1,128)S(1)} %bitcast.33), channel_id=1, replica_groups=mesh['y'=2,'core'=2,'col'=8] {'y','core','col'}, dimensions={0} | all-to-all | bytes 32768 | tf_op jit(solution)/shard_map/all_to_all | solution.py:300
  50.5 0.0 collective-permute-done.5.got_2
  50.5 0.0 collective-permute-done.6.got_1
  50.5 0.0 collective-permute-done.7.got_0
  50.5 0.0 collective-permute-done.8.got_3
  50.5 0.0 copy-done
  50.5 0.0 copy-done.1
  50.5 1.7 %update.1 = (f32[16,128,128]{2,1,0:T(8,128)}, f32[16,128,128]{2,1,0:T(8,128)}) custom-call(s32[4,4]{1,0:T(4,128)S(1)} %bitcast.32, f32[16,128,128]{2,1,0:T(8,128)S(1)} %bitcast.24, f32[16,128,128]{2,1,0:T(8,128)S(1)} %bitcast.23, f32[16,128,128]{2,1,0:T(8,128)S(1)} %get-tuple-element.30.direction, f32[16,128,128]{2,1,0:T(8,128)S(1)} %get-tuple-element.31.image, ...), custom_call_target="tpu_custom_call" | custom-call | tf_op jit(solution)/shard_map/update/pallas_call | solution.py:426
Async XLA Ops:
  5.0 17.1 %all-to-all-start = ((f32[16,1,3328]{2,1,0:T(1,128)}), f32[16,1,3328]{2,1,0:T(1,128)S(1)}, u32[]{:S(2)}, u32[]{:S(2)}) async-start(f32[16,1,3328]{2,1,0:T(1,128)} %bitcast.10), calls=%async_computation | async-start | bytes 425984 | tf_op jit(solution)/shard_map/all_to_all | solution.py:300
  13.3 13.6 %collective-permute-start.1 = (f32[544,128]{1,0:T(8,128)S(1)}, f32[544,128]{1,0:T(8,128)S(1)}, u32[]{:S(2)}, u32[]{:S(2)}) collective-permute-start(f32[544,128]{1,0:T(8,128)S(1)} %get-tuple-element.26), channel_id=1, source_target_pairs={{0,1},{2,3},{4,5},{6,7},{1,0},{3,2},{5,4},{7,6},{8,9},{10,11},{12,... | collective-permute-start | bytes 835592 | tf_op jit(solution)/shard_map/ppermute | solution.py:295
  15.2 11.7 %collective-permute-start.2 = (f32[544,128]{1,0:T(8,128)S(1)}, f32[544,128]{1,0:T(8,128)S(1)}, u32[]{:S(2)}, u32[]{:S(2)}) collective-permute-start(f32[544,128]{1,0:T(8,128)S(1)} %get-tuple-element.27), channel_id=1, source_target_pairs={{8,16},{16,8},{9,17},{17,9},{10,18},{18,10},{11,19},{19,11},{12,20... | collective-permute-start | bytes 835592 | tf_op jit(solution)/shard_map/ppermute | solution.py:295
  15.9 11.0 %collective-permute-start.3 = (f32[544,128]{1,0:T(8,128)S(1)}, f32[544,128]{1,0:T(8,128)S(1)}, u32[]{:S(2)}, u32[]{:S(2)}) collective-permute-start(f32[544,128]{1,0:T(8,128)S(1)} %get-tuple-element.28), channel_id=1, source_target_pairs={{0,8},{16,24},{8,0},{24,16},{1,9},{17,25},{9,1},{25,17},{2,10},{18... | collective-permute-start | bytes 835592 | tf_op jit(solution)/shard_map/ppermute | solution.py:295
  18.8 8.2 %collective-permute-start.4 = (f32[544,128]{1,0:T(8,128)S(1)}, f32[544,128]{1,0:T(8,128)S(1)}, u32[]{:S(2)}, u32[]{:S(2)}) collective-permute-start(f32[544,128]{1,0:T(8,128)S(1)} %get-tuple-element.29), channel_id=1, source_target_pairs={{1,2},{3,4},{5,6},{2,1},{4,3},{6,5},{9,10},{11,12},{13,14},{10,9},... | collective-permute-start | bytes 835592 | tf_op jit(solution)/shard_map/ppermute | solution.py:295
  22.1 2.1 %collective-permute-start = (f32[416,128]{1,0:T(8,128)S(1)}, f32[416,128]{1,0:T(8,128)S(1)}, u32[]{:S(2)}, u32[]{:S(2)}) collective-permute-start(f32[416,128]{1,0:T(8,128)S(1)} %bitcast.25), channel_id=1, source_target_pairs={{0,8},{8,0},{1,9},{9,1},{2,10},{10,2},{3,11},{11,3},{4,12},{12,4},... | collective-permute-start | bytes 638984 | tf_op jit(solution)/shard_map/ppermute | solution.py:370
  22.1 2.1 %copy-start.2 = (f32[1,1,8,2048]{3,2,1,0:T(8,128)S(1)}, f32[1,1,8,2048]{3,2,1,0:T(8,128)}, u32[]{:S(2)}) copy-start(f32[1,1,8,2048]{3,2,1,0:T(8,128)} %param.21) | copy-start | bytes 196612
  22.1 2.1 %copy-start.5 = (s32[1,1,16]{2,1,0:T(1,128)S(1)}, s32[1,1,16]{2,1,0:T(1,128)}, u32[]{:S(2)}) copy-start(s32[1,1,16]{2,1,0:T(1,128)} %param.17) | copy-start | bytes 196
  22.1 2.1 %copy-start.6 = (s32[1,1,8]{2,1,0:T(1,128)S(1)}, s32[1,1,8]{2,1,0:T(1,128)}, u32[]{:S(2)}) copy-start(s32[1,1,8]{2,1,0:T(1,128)} %param.22) | copy-start | bytes 100
  22.1 2.1 %copy-start.7 = (f32[128]{0:T(128)S(1)}, f32[128]{0:T(128)}, u32[]{:S(2)}) copy-start(f32[128]{0:T(128)} %param.15) | copy-start | bytes 1540
  22.1 4.9 %copy-start.3 = (s32[1,1,4,4]{3,2,1,0:T(4,128)S(1)}, s32[1,1,4,4]{3,2,1,0:T(4,128)}, u32[]{:S(2)}) copy-start(s32[1,1,4,4]{3,2,1,0:T(4,128)} %param.16) | copy-start | bytes 196
  22.1 4.9 %copy-start.4 = (s32[1,1,16,3]{2,1,3,0:T(1,128)S(1)}, s32[1,1,16,3]{2,1,3,0:T(1,128)}, u32[]{:S(2)}) copy-start(s32[1,1,16,3]{2,1,3,0:T(1,128)} %param.18) | copy-start | bytes 580
  26.9 23.6 %copy-start = (f32[1,1,16,128,128]{4,3,2,1,0:T(8,128)S(1)}, f32[1,1,16,128,128]{4,3,2,1,0:T(8,128)}, u32[]{:S(2)}) copy-start(f32[1,1,16,128,128]{4,3,2,1,0:T(8,128)} %param.13) | copy-start | bytes 3145732
  26.9 23.6 %copy-start.1 = (f32[1,1,16,128,128]{4,3,2,1,0:T(8,128)S(1)}, f32[1,1,16,128,128]{4,3,2,1,0:T(8,128)}, u32[]{:S(2)}) copy-start(f32[1,1,16,128,128]{4,3,2,1,0:T(8,128)} %param.12) | copy-start | bytes 3145732
  29.5 20.9 %collective-permute-start.5 = (f32[512,128]{1,0:T(8,128)S(1)}, f32[512,128]{1,0:T(8,128)S(1)}, u32[]{:S(2)}, u32[]{:S(2)}) collective-permute-start(f32[512,128]{1,0:T(8,128)S(1)} %get-tuple-element.32), channel_id=1, source_target_pairs={{0,1},{2,3},{4,5},{6,7},{1,0},{3,2},{5,4},{7,6},{8,9},{10,11},{12,... | collective-permute-start | bytes 786440 | tf_op jit(solution)/shard_map/ppermute | solution.py:295
  33.6 16.9 %collective-permute-start.6 = (f32[512,128]{1,0:T(8,128)S(1)}, f32[512,128]{1,0:T(8,128)S(1)}, u32[]{:S(2)}, u32[]{:S(2)}) collective-permute-start(f32[512,128]{1,0:T(8,128)S(1)} %get-tuple-element.33), channel_id=1, source_target_pairs={{8,16},{16,8},{9,17},{17,9},{10,18},{18,10},{11,19},{19,11},{12,20... | collective-permute-start | bytes 786440 | tf_op jit(solution)/shard_map/ppermute | solution.py:295
  34.3 16.2 %collective-permute-start.7 = (f32[512,128]{1,0:T(8,128)S(1)}, f32[512,128]{1,0:T(8,128)S(1)}, u32[]{:S(2)}, u32[]{:S(2)}) collective-permute-start(f32[512,128]{1,0:T(8,128)S(1)} %get-tuple-element.34), channel_id=1, source_target_pairs={{0,8},{16,24},{8,0},{24,16},{1,9},{17,25},{9,1},{25,17},{2,10},{18... | collective-permute-start | bytes 786440 | tf_op jit(solution)/shard_map/ppermute | solution.py:295
  37.2 13.2 %collective-permute-start.8 = (f32[512,128]{1,0:T(8,128)S(1)}, f32[512,128]{1,0:T(8,128)S(1)}, u32[]{:S(2)}, u32[]{:S(2)}) collective-permute-start(f32[512,128]{1,0:T(8,128)S(1)} %get-tuple-element.35), channel_id=1, source_target_pairs={{1,2},{3,4},{5,6},{2,1},{4,3},{6,5},{9,10},{11,12},{13,14},{10,9},... | collective-permute-start | bytes 786440 | tf_op jit(solution)/shard_map/ppermute | solution.py:295
where the time goes:
time: 52.5 us; the launch traced here: 52.2 us
  starting transfers between devices  22.8 us (43%)
  Pallas kernels  13.3 us (25%)
  blocking collectives  12.6 us (24%)
  waiting for transfers between devices  2.64 us (5%)
  between operations  0.87 us (2%)
    ppermute x8, starting transfers between devices, swap_pairs(): return lax.ppermute(x, axis, pairs + [(j, i) for i, j in pairs])  14.5 us
    all_to_all x1, blocking collectives, from_all(): lax.all_to_all(sent, axes, split_axis=0, concat_axis=0, tiled=True)  12.6 us
    all_to_all x1, starting transfers between devices, from_all(): lax.all_to_all(sent, axes, split_axis=0, concat_axis=0, tiled=True)  8.32 us
    pallas_call x1, Pallas kernels, per_device(): pl.pallas_call(local_kernel, out_shape=(held(count, dofs, cases), face, s...  4.32 us
    pallas_call x1, Pallas kernels, per_device(): pl.pallas_call(coarse_kernel, out_shape=(held(count, dofs, cases), held(3...  2.65 us
    all_to_all x1, waiting for transfers between devices, from_all(): lax.all_to_all(sent, axes, split_axis=0, concat_axis=0, tiled=True)  2.62 us
    pallas_call x1, Pallas kernels, per_device(): pl.pallas_call(direction_kernel, out_shape=(shape(count, dofs, cases), he...  2.56 us
    pallas_call x1, Pallas kernels, per_device(): pl.pallas_call(halving_kernel, out_shape=pltpu.VMEM((count, 2 * dofs, 3 *...  2.06 us
  transfers between devices with their start and end apart: 10, of which 1 were waited for; matrix products, arithmetic and copies ran while one was open for 0% of the time, Pallas kernels for 9%

commit v1 on v0

--- a/solution.py
+++ b/solution.py
@@ -107,7 +107,7 @@
     for c, (start, stop) in enumerate(((0, count // 4), (count // 4, count))):
         part = pl.ds(start, stop - start)
         neumann_copies[start] = pltpu.make_async_copy(neumann_hbm.at[part], neumann.at[part], neumann_sems.at[c])
-    for copy in (*index_copies, residual_copy, basis_copy, *neumann_copies.values(), inverse_copy):
+    for copy in (*index_copies, residual_copy, basis_copy, inverse_copy, *neumann_copies.values()):
         copy.start()
     for copy in index_copies:
         copy.wait()
@@ -120,6 +120,7 @@
         if b in neumann_copies:
             neumann_copies[b].wait()
         if b == count // 4:
+            inverse_copy.wait()
             coarse_local = product(basis[...], pairs[...].reshape(count * 128, 256))
         weight = weight_of(multiplicity, b)
         out = row_product(halved_rows(neumann.at[b]), pattern, b, pairs) * weight
@@ -128,7 +129,6 @@
     row = lax.broadcasted_iota(jnp.int32, (8, 128), 0)
     total = jnp.sum(total, axis=0, keepdims=True)
     map_row = mapped(primal_map, (8, 128), 1).astype(F32)
-    inverse_copy.wait()
     sharers = inverse.shape[0] // 8
     mine = row_index() % sharers
     share = inverse[pl.ds(pl.multiple_of(mine * 8, 8), 8), :]

time: 52.5 us -> 52.6 us (level)
  no operation moved by 1% of the time
where the time goes in v1:
time: 52.6 us; the launch traced here: 52.2 us
  starting transfers between devices  22.8 us (43%)
  Pallas kernels  13.3 us (25%)
  blocking collectives  12.6 us (24%)
  waiting for transfers between devices  2.64 us (5%)
  between operations  0.87 us (2%)
    ppermute x8, starting transfers between devices, swap_pairs(): return lax.ppermute(x, axis, pairs + [(j, i) for i, j in pairs])  14.5 us
    all_to_all x1, blocking collectives, from_all(): lax.all_to_all(sent, axes, split_axis=0, concat_axis=0, tiled=True)  12.6 us
    all_to_all x1, starting transfers between devices, from_all(): lax.all_to_all(sent, axes, split_axis=0, concat_axis=0, tiled=True)  8.32 us
    pallas_call x1, Pallas kernels, per_device(): pl.pallas_call(local_kernel, out_shape=(held(count, dofs, cases), face, s...  4.32 us
    pallas_call x1, Pallas kernels, per_device(): pl.pallas_call(coarse_kernel, out_shape=(held(count, dofs, cases), held(3...  2.64 us
    all_to_all x1, waiting for transfers between devices, from_all(): lax.all_to_all(sent, axes, split_axis=0, concat_axis=0, tiled=True)  2.62 us
    pallas_call x1, Pallas kernels, per_device(): pl.pallas_call(direction_kernel, out_shape=(shape(count, dofs, cases), he...  2.56 us
    pallas_call x1, Pallas kernels, per_device(): pl.pallas_call(halving_kernel, out_shape=pltpu.VMEM((count, 2 * dofs, 3 *...  2.06 us
  transfers between devices with their start and end apart: 10, of which 1 were waited for; matrix products, arithmetic and copies ran while one was open for 0% of the time, Pallas kernels for 9%

profile of v1, /device:TPU:0, one launch (start us, length us, event | category | flops | bytes accessed | tf_op | source)
XLA Modules:
  0.0 52.2 jit_solution(8169439604376320257)
XLA Ops:
  0.6 4.3 %local_solve.1 = (f32[16,128,128]{2,1,0:T(8,128)S(1)}, f32[544,128]{1,0:T(8,128)S(1)}, f32[416,128]{1,0:T(8,128)}, f32[544,128]{1,0:T(8,128)S(1)}, f32[544,128]{1,0:T(8,128)S(1)}, /*index=5*/f32[544,128]{1,0:T(8,128)S(1)}) custom-call(s32[4,4]{1,0:T(4,128)} %bitcast.30, s32[16]{0:T(128)} %bitcast.36, s32[3,1,16]{2,1,0:T(1,128)} %bitcast.34, s32[8]{0:T(128)} %bitcast.38, ...), custom_call_target="tpu_custom_call" | custom-call | tf_op jit(solution)/shard_map/local_solve/pallas_call | solution.py:346
  5.0 8.3 %all-to-all-start = ((f32[16,1,3328]{2,1,0:T(1,128)}), f32[16,1,3328]{2,1,0:T(1,128)S(1)}, u32[]{:S(2)}, u32[]{:S(2)}) async-start(f32[16,1,3328]{2,1,0:T(1,128)} %bitcast.10), calls=%async_computation | async-start | bytes 425984 | tf_op jit(solution)/shard_map/all_to_all | solution.py:300
  13.3 1.9 %collective-permute-start.1 = (f32[544,128]{1,0:T(8,128)S(1)}, f32[544,128]{1,0:T(8,128)S(1)}, u32[]{:S(2)}, u32[]{:S(2)}) collective-permute-start(f32[544,128]{1,0:T(8,128)S(1)} %get-tuple-element.26), channel_id=1, source_target_pairs={{0,1},{2,3},{4,5},{6,7},{1,0},{3,2},{5,4},{7,6},{8,9},{10,11},{12,... | collective-permute-start | bytes 835592 | tf_op jit(solution)/shard_map/ppermute | solution.py:295
  15.2 0.7 %collective-permute-start.2 = (f32[544,128]{1,0:T(8,128)S(1)}, f32[544,128]{1,0:T(8,128)S(1)}, u32[]{:S(2)}, u32[]{:S(2)}) collective-permute-start(f32[544,128]{1,0:T(8,128)S(1)} %get-tuple-element.27), channel_id=1, source_target_pairs={{8,16},{16,8},{9,17},{17,9},{10,18},{18,10},{11,19},{19,11},{12,20... | collective-permute-start | bytes 835592 | tf_op jit(solution)/shard_map/ppermute | solution.py:295
  15.9 2.9 %collective-permute-start.3 = (f32[544,128]{1,0:T(8,128)S(1)}, f32[544,128]{1,0:T(8,128)S(1)}, u32[]{:S(2)}, u32[]{:S(2)}) collective-permute-start(f32[544,128]{1,0:T(8,128)S(1)} %get-tuple-element.28), channel_id=1, source_target_pairs={{0,8},{16,24},{8,0},{24,16},{1,9},{17,25},{9,1},{25,17},{2,10},{18... | collective-permute-start | bytes 835592 | tf_op jit(solution)/shard_map/ppermute | solution.py:295
  18.8 0.7 %collective-permute-start.4 = (f32[544,128]{1,0:T(8,128)S(1)}, f32[544,128]{1,0:T(8,128)S(1)}, u32[]{:S(2)}, u32[]{:S(2)}) collective-permute-start(f32[544,128]{1,0:T(8,128)S(1)} %get-tuple-element.29), channel_id=1, source_target_pairs={{1,2},{3,4},{5,6},{2,1},{4,3},{6,5},{9,10},{11,12},{13,14},{10,9},... | collective-permute-start | bytes 835592 | tf_op jit(solution)/shard_map/ppermute | solution.py:295
  19.4 2.6 %all-to-all-done = f32[16,1,3328]{2,1,0:T(1,128)S(1)} async-done(((f32[16,1,3328]{2,1,0:T(1,128)}), f32[16,1,3328]{2,1,0:T(1,128)S(1)}, u32[]{:S(2)}, u32[]{:S(2)}) %all-to-all-start) | async-done | bytes 213024 | tf_op jit(solution)/shard_map/all_to_all | solution.py:300
  22.1 0.0 collective-permute-start
  22.1 0.0 copy-start.2
  22.1 0.0 copy-start.5
  22.1 0.0 copy-start.6
  22.1 0.0 copy-start.7
  22.1 0.0 copy-start.3
  22.1 0.0 copy-start.4
  22.1 2.1 %halving.1.stacked = bf16[16,256,384]{2,1,0:T(8,128)(2,1)S(1)} custom-call(f32[16,3,128,128]{3,2,1,0:T(8,128)} %bitcast.41), custom_call_target="tpu_custom_call" | custom-call | tf_op jit(solution)/shard_map/halving/pallas_call | solution.py:376
  24.2 0.0 collective-permute-done.other_core
  24.2 0.0 copy-done.2
  24.2 0.0 copy-done.5
  24.2 0.0 copy-done.6
  24.2 0.0 copy-done.7
  24.2 2.6 %coarse_solve.1 = (f32[16,128,128]{2,1,0:T(8,128)S(1)}, f32[32,128]{1,0:T(8,128)S(1)}, f32[1,128]{1,0:T(1,128)S(1)}) custom-call(s32[16]{0:T(128)S(1)} %bitcast.37, s32[8]{0:T(128)S(1)} %bitcast.39, f32[16,128,128]{2,1,0:T(8,128)S(1)} %get-tuple-element.22.local, f32[416,128]{1,0:T(8,128)S(1)} %bitcast.26, f32[416,128]{1,0:T(8,128)S(1)} %collective-permute-done.other_core, ...), custom_call_target="tpu_custom_call" | custom-call | tf_op jit(solution)/shard_map/coarse_solve/pallas_call | solution.py:386
  26.9 0.0 copy-start
  26.9 0.0 copy-start.1
  26.9 0.0 collective-permute-done.1.got_2
  26.9 0.0 collective-permute-done.2.got_1
  26.9 0.0 collective-permute-done.3.got_0
  26.9 0.0 collective-permute-done.4.got_3
  26.9 0.0 copy-done.3
  27.0 0.0 copy-done.4
  27.0 2.6 %direction_image.1 = (f32[16,128,128]{2,1,0:T(8,128)}, f32[16,128,128]{2,1,0:T(8,128)S(1)}, f32[16,128,128]{2,1,0:T(8,128)S(1)}, f32[512,128]{1,0:T(8,128)S(1)},...) custom-call(s32[4,4]{1,0:T(4,128)S(1)} %bitcast.31, ...), custom_call_target="tpu_custom_call" | custom-call | tf_op jit(solution)/shard_map/direction_image/pallas_call | solution.py:403
  29.5 4.1 %collective-permute-start.5 = (f32[512,128]{1,0:T(8,128)S(1)}, f32[512,128]{1,0:T(8,128)S(1)}, u32[]{:S(2)}, u32[]{:S(2)}) collective-permute-start(f32[512,128]{1,0:T(8,128)S(1)} %get-tuple-element.32), channel_id=1, source_target_pairs={{0,1},{2,3},{4,5},{6,7},{1,0},{3,2},{5,4},{7,6},{8,9},{10,11},{12,... | collective-permute-start | bytes 786440 | tf_op jit(solution)/shard_map/ppermute | solution.py:295
  33.6 0.7 %collective-permute-start.6 = (f32[512,128]{1,0:T(8,128)S(1)}, f32[512,128]{1,0:T(8,128)S(1)}, u32[]{:S(2)}, u32[]{:S(2)}) collective-permute-start(f32[512,128]{1,0:T(8,128)S(1)} %get-tuple-element.33), channel_id=1, source_target_pairs={{8,16},{16,8},{9,17},{17,9},{10,18},{18,10},{11,19},{19,11},{12,20... | collective-permute-start | bytes 786440 | tf_op jit(solution)/shard_map/ppermute | solution.py:295
  34.3 3.0 %collective-permute-start.7 = (f32[512,128]{1,0:T(8,128)S(1)}, f32[512,128]{1,0:T(8,128)S(1)}, u32[]{:S(2)}, u32[]{:S(2)}) collective-permute-start(f32[512,128]{1,0:T(8,128)S(1)} %get-tuple-element.34), channel_id=1, source_target_pairs={{0,8},{16,24},{8,0},{24,16},{1,9},{17,25},{9,1},{25,17},{2,10},{18... | collective-permute-start | bytes 786440 | tf_op jit(solution)/shard_map/ppermute | solution.py:295
  37.2 0.7 %collective-permute-start.8 = (f32[512,128]{1,0:T(8,128)S(1)}, f32[512,128]{1,0:T(8,128)S(1)}, u32[]{:S(2)}, u32[]{:S(2)}) collective-permute-start(f32[512,128]{1,0:T(8,128)S(1)} %get-tuple-element.35), channel_id=1, source_target_pairs={{1,2},{3,4},{5,6},{2,1},{4,3},{6,5},{9,10},{11,12},{13,14},{10,9},... | collective-permute-start | bytes 786440 | tf_op jit(solution)/shard_map/ppermute | solution.py:295
  37.9 12.6 %all_to_all.10 = f32[32,1,128]{2,1,0:T(1,128)S(1)} all-to-all(f32[32,1,128]{2,1,0:T(1,128)S(1)} %bitcast.33), channel_id=1, replica_groups=mesh['y'=2,'core'=2,'col'=8] {'y','core','col'}, dimensions={0} | all-to-all | bytes 32768 | tf_op jit(solution)/shard_map/all_to_all | solution.py:300
  50.5 0.0 collective-permute-done.5.got_2
  50.5 0.0 collective-permute-done.6.got_1
  50.5 0.0 collective-permute-done.7.got_0
  50.5 0.0 collective-permute-done.8.got_3
  50.5 0.0 copy-done
  50.5 0.0 copy-done.1
  50.5 1.7 %update.1 = (f32[16,128,128]{2,1,0:T(8,128)}, f32[16,128,128]{2,1,0:T(8,128)}) custom-call(s32[4,4]{1,0:T(4,128)S(1)} %bitcast.32, f32[16,128,128]{2,1,0:T(8,128)S(1)} %bitcast.24, f32[16,128,128]{2,1,0:T(8,128)S(1)} %bitcast.23, f32[16,128,128]{2,1,0:T(8,128)S(1)} %get-tuple-element.30.direction, f32[16,128,128]{2,1,0:T(8,128)S(1)} %get-tuple-element.31.image, ...), custom_call_target="tpu_custom_call" | custom-call | tf_op jit(solution)/shard_map/update/pallas_call | solution.py:426
Async XLA Ops:
  5.0 17.1 %all-to-all-start = ((f32[16,1,3328]{2,1,0:T(1,128)}), f32[16,1,3328]{2,1,0:T(1,128)S(1)}, u32[]{:S(2)}, u32[]{:S(2)}) async-start(f32[16,1,3328]{2,1,0:T(1,128)} %bitcast.10), calls=%async_computation | async-start | bytes 425984 | tf_op jit(solution)/shard_map/all_to_all | solution.py:300
  13.3 13.6 %collective-permute-start.1 = (f32[544,128]{1,0:T(8,128)S(1)}, f32[544,128]{1,0:T(8,128)S(1)}, u32[]{:S(2)}, u32[]{:S(2)}) collective-permute-start(f32[544,128]{1,0:T(8,128)S(1)} %get-tuple-element.26), channel_id=1, source_target_pairs={{0,1},{2,3},{4,5},{6,7},{1,0},{3,2},{5,4},{7,6},{8,9},{10,11},{12,... | collective-permute-start | bytes 835592 | tf_op jit(solution)/shard_map/ppermute | solution.py:295
  15.2 11.7 %collective-permute-start.2 = (f32[544,128]{1,0:T(8,128)S(1)}, f32[544,128]{1,0:T(8,128)S(1)}, u32[]{:S(2)}, u32[]{:S(2)}) collective-permute-start(f32[544,128]{1,0:T(8,128)S(1)} %get-tuple-element.27), channel_id=1, source_target_pairs={{8,16},{16,8},{9,17},{17,9},{10,18},{18,10},{11,19},{19,11},{12,20... | collective-permute-start | bytes 835592 | tf_op jit(solution)/shard_map/ppermute | solution.py:295
  15.9 11.0 %collective-permute-start.3 = (f32[544,128]{1,0:T(8,128)S(1)}, f32[544,128]{1,0:T(8,128)S(1)}, u32[]{:S(2)}, u32[]{:S(2)}) collective-permute-start(f32[544,128]{1,0:T(8,128)S(1)} %get-tuple-element.28), channel_id=1, source_target_pairs={{0,8},{16,24},{8,0},{24,16},{1,9},{17,25},{9,1},{25,17},{2,10},{18... | collective-permute-start | bytes 835592 | tf_op jit(solution)/shard_map/ppermute | solution.py:295
  18.8 8.2 %collective-permute-start.4 = (f32[544,128]{1,0:T(8,128)S(1)}, f32[544,128]{1,0:T(8,128)S(1)}, u32[]{:S(2)}, u32[]{:S(2)}) collective-permute-start(f32[544,128]{1,0:T(8,128)S(1)} %get-tuple-element.29), channel_id=1, source_target_pairs={{1,2},{3,4},{5,6},{2,1},{4,3},{6,5},{9,10},{11,12},{13,14},{10,9},... | collective-permute-start | bytes 835592 | tf_op jit(solution)/shard_map/ppermute | solution.py:295
  22.1 2.1 %collective-permute-start = (f32[416,128]{1,0:T(8,128)S(1)}, f32[416,128]{1,0:T(8,128)S(1)}, u32[]{:S(2)}, u32[]{:S(2)}) collective-permute-start(f32[416,128]{1,0:T(8,128)S(1)} %bitcast.25), channel_id=1, source_target_pairs={{0,8},{8,0},{1,9},{9,1},{2,10},{10,2},{3,11},{11,3},{4,12},{12,4},... | collective-permute-start | bytes 638984 | tf_op jit(solution)/shard_map/ppermute | solution.py:370
  22.1 2.1 %copy-start.2 = (f32[1,1,8,2048]{3,2,1,0:T(8,128)S(1)}, f32[1,1,8,2048]{3,2,1,0:T(8,128)}, u32[]{:S(2)}) copy-start(f32[1,1,8,2048]{3,2,1,0:T(8,128)} %param.21) | copy-start | bytes 196612
  22.1 2.1 %copy-start.5 = (s32[1,1,16]{2,1,0:T(1,128)S(1)}, s32[1,1,16]{2,1,0:T(1,128)}, u32[]{:S(2)}) copy-start(s32[1,1,16]{2,1,0:T(1,128)} %param.17) | copy-start | bytes 196
  22.1 2.1 %copy-start.6 = (s32[1,1,8]{2,1,0:T(1,128)S(1)}, s32[1,1,8]{2,1,0:T(1,128)}, u32[]{:S(2)}) copy-start(s32[1,1,8]{2,1,0:T(1,128)} %param.22) | copy-start | bytes 100
  22.1 2.1 %copy-start.7 = (f32[128]{0:T(128)S(1)}, f32[128]{0:T(128)}, u32[]{:S(2)}) copy-start(f32[128]{0:T(128)} %param.15) | copy-start | bytes 1540
  22.1 4.9 %copy-start.3 = (s32[1,1,4,4]{3,2,1,0:T(4,128)S(1)}, s32[1,1,4,4]{3,2,1,0:T(4,128)}, u32[]{:S(2)}) copy-start(s32[1,1,4,4]{3,2,1,0:T(4,128)} %param.16) | copy-start | bytes 196
  22.1 4.9 %copy-start.4 = (s32[1,1,16,3]{2,1,3,0:T(1,128)S(1)}, s32[1,1,16,3]{2,1,3,0:T(1,128)}, u32[]{:S(2)}) copy-start(s32[1,1,16,3]{2,1,3,0:T(1,128)} %param.18) | copy-start | bytes 580
  26.9 23.6 %copy-start = (f32[1,1,16,128,128]{4,3,2,1,0:T(8,128)S(1)}, f32[1,1,16,128,128]{4,3,2,1,0:T(8,128)}, u32[]{:S(2)}) copy-start(f32[1,1,16,128,128]{4,3,2,1,0:T(8,128)} %param.13) | copy-start | bytes 3145732
  26.9 23.6 %copy-start.1 = (f32[1,1,16,128,128]{4,3,2,1,0:T(8,128)S(1)}, f32[1,1,16,128,128]{4,3,2,1,0:T(8,128)}, u32[]{:S(2)}) copy-start(f32[1,1,16,128,128]{4,3,2,1,0:T(8,128)} %param.12) | copy-start | bytes 3145732
  29.5 20.9 %collective-permute-start.5 = (f32[512,128]{1,0:T(8,128)S(1)}, f32[512,128]{1,0:T(8,128)S(1)}, u32[]{:S(2)}, u32[]{:S(2)}) collective-permute-start(f32[512,128]{1,0:T(8,128)S(1)} %get-tuple-element.32), channel_id=1, source_target_pairs={{0,1},{2,3},{4,5},{6,7},{1,0},{3,2},{5,4},{7,6},{8,9},{10,11},{12,... | collective-permute-start | bytes 786440 | tf_op jit(solution)/shard_map/ppermute | solution.py:295
  33.6 16.9 %collective-permute-start.6 = (f32[512,128]{1,0:T(8,128)S(1)}, f32[512,128]{1,0:T(8,128)S(1)}, u32[]{:S(2)}, u32[]{:S(2)}) collective-permute-start(f32[512,128]{1,0:T(8,128)S(1)} %get-tuple-element.33), channel_id=1, source_target_pairs={{8,16},{16,8},{9,17},{17,9},{10,18},{18,10},{11,19},{19,11},{12,20... | collective-permute-start | bytes 786440 | tf_op jit(solution)/shard_map/ppermute | solution.py:295
  34.3 16.2 %collective-permute-start.7 = (f32[512,128]{1,0:T(8,128)S(1)}, f32[512,128]{1,0:T(8,128)S(1)}, u32[]{:S(2)}, u32[]{:S(2)}) collective-permute-start(f32[512,128]{1,0:T(8,128)S(1)} %get-tuple-element.34), channel_id=1, source_target_pairs={{0,8},{16,24},{8,0},{24,16},{1,9},{17,25},{9,1},{25,17},{2,10},{18... | collective-permute-start | bytes 786440 | tf_op jit(solution)/shard_map/ppermute | solution.py:295
  37.2 13.2 %collective-permute-start.8 = (f32[512,128]{1,0:T(8,128)S(1)}, f32[512,128]{1,0:T(8,128)S(1)}, u32[]{:S(2)}, u32[]{:S(2)}) collective-permute-start(f32[512,128]{1,0:T(8,128)S(1)} %get-tuple-element.35), channel_id=1, source_target_pairs={{1,2},{3,4},{5,6},{2,1},{4,3},{6,5},{9,10},{11,12},{13,14},{10,9},... | collective-permute-start | bytes 786440 | tf_op jit(solution)/shard_map/ppermute | solution.py:295
